TPU v7x, 512 devices: a whole 4x4x16 slice. The times are simulated.
512 devices in a mesh: dp: 16 (over y, z_hi), mod: 32 (over x, z_lo, core).
Axes of the slice: x: 4, y: 4, z: 16 (z_hi: 4, z_lo: 4; z = z_hi * 4 + z_lo), core: 2. Of those that a mesh axis runs over, the one named last changes fastest.
Arguments:
- normed_states: bfloat16 [65536, 8192], P(('dp', 'mod')), may hold values from -6 to 6
- kv_cotangent: bfloat16 [65536, 512], P(('dp', 'mod')), may hold values from -6 to 6
- token_types: int32 [65536, 1], P(('dp', 'mod')), may hold values from 0 to 1; in each aligned block of 128 rows (0 to 127, 128 to 255, ...) at most 96 rows name the same one
- kv_weight: bfloat16 [16384, 512], P('mod'), may hold values from -0.25 to 0.25
Outputs:
- state_grad: bfloat16 [65536, 8192], P(('dp', 'mod'))
- kv_weight_grad: float32 [16384, 512], P(('mod', 'dp'))
Inputs may be any that keep to these rules, and one draw needn't show every extreme that they name: `token_types`: in each aligned block of 128 rows (the rows of one device) at most 96 rows name the same modality; in every draw some block has exactly 96 rows of one modality.
All inputs are finite; a program needn't handle non-finite values.
Results may differ from a plain program's by a relative error of at most 0.001.
Values may be sent and summed in bfloat16 or wider, within the bound.
A program may use at most 128 MiB of HBM per device.

v0:
```python
import math

import jax
import jax.numpy as jnp
from jax import lax
from jax.sharding import PartitionSpec as P


def compact_tables(row_kinds, capacity):
    placers = []
    for modality in range(2):
        member = (row_kinds == modality).astype(jnp.float32)
        ordinal = jnp.cumsum(member) - 1.0
        slot_iota = lax.broadcasted_iota(jnp.float32, (capacity, row_kinds.shape[0]), 0)
        placer = jnp.where((ordinal[None, :] == slot_iota) & (member[None, :] > 0.0), 1.0, 0.0)
        placers.append(placer.astype(jnp.bfloat16))
    return placers


def body(normed_states, kv_cotangent, token_types, kv_weight):
    devices_mod = lax.axis_size("mod")
    devices_dp = lax.axis_size("dp")
    owner_count = devices_mod // 2
    slice_width = kv_weight.shape[0]
    tok_rows = normed_states.shape[0]
    kv_width = kv_cotangent.shape[1]
    row_kinds = token_types[:, 0]
    split_states = normed_states.reshape(tok_rows, owner_count, slice_width)
    contract_cols = (((1,), (1,)), ((), ()))
    contract_rows = (((0,), (0,)), ((), ()))
    capacity = 3 * tok_rows // 4
    placers = compact_tables(row_kinds, capacity)
    state_parts = []
    grad_parts = []
    for placer in placers:
        packed_states = jnp.einsum(
            "ct,ths->hcs", placer, split_states, preferred_element_type=jnp.float32
        )
        state_parts.append(packed_states.astype(jnp.bfloat16))
        packed_grads = jnp.dot(placer, kv_cotangent, preferred_element_type=jnp.float32).astype(
            jnp.bfloat16
        )
        grad_parts.append(jnp.broadcast_to(packed_grads[None], (owner_count, capacity, kv_width)))
    states_send = jnp.concatenate(state_parts, 0)
    grads_send = jnp.concatenate(grad_parts, 0)
    states_recv, grads_recv = (
        lax.all_to_all(states_send, "mod", split_axis=0, concat_axis=0, tiled=True),
        lax.all_to_all(grads_send, "mod", split_axis=0, concat_axis=0, tiled=True),
    )
    input_rows = states_recv.reshape(devices_mod * capacity, slice_width)
    output_rows = grads_recv.reshape(devices_mod * capacity, kv_width)
    partial_dx = lax.dot_general(
        output_rows, kv_weight, contract_cols, preferred_element_type=jnp.float32
    ).astype(jnp.bfloat16)
    returned = lax.all_to_all(
        partial_dx.reshape(devices_mod, capacity, slice_width),
        "mod",
        split_axis=0,
        concat_axis=0,
        tiled=True,
    )
    returned = returned.reshape(2, owner_count, capacity, slice_width)
    unpacked = jnp.einsum(
        "ct,hcs->ths", placers[0], returned[0], preferred_element_type=jnp.float32
    )
    unpacked = unpacked + jnp.einsum(
        "ct,hcs->ths", placers[1], returned[1], preferred_element_type=jnp.float32
    )
    state_grad = unpacked.reshape(tok_rows, owner_count * slice_width).astype(jnp.bfloat16)
    grad_scale = 1.0 / math.sqrt(tok_rows * devices_mod * devices_dp)
    summed = lax.psum_scatter(
        lax.dot_general(input_rows, output_rows, contract_rows, preferred_element_type=jnp.float32),
        "dp",
        scatter_dimension=0,
        tiled=True,
    )
    return (state_grad, summed * grad_scale)


def solution(mesh):
    in_specs = (
        P(("dp", "mod"), None),
        P(("dp", "mod"), None),
        P(("dp", "mod"), None),
        P("mod", None),
    )
    out_specs = (P(("dp", "mod"), None), P(("mod", "dp"), None))
    return jax.shard_map(body, mesh=mesh, in_specs=in_specs, out_specs=out_specs, check_vma=False)
```

profile of v0, /device:TPU:6, one launch (start us, length us, event | category | flops | bytes accessed | tf_op | source)
XLA Modules:
  0.0 334.1 jit_solution(5316758563596502279)
XLA Ops:
  7.2 0.0 copy-start
  7.2 0.7 compare_bitcast_fusion.1
  7.9 0.1 copy.9
  8.0 0.2 reduce-window.17
  8.2 0.1 add_reduce_fusion
  8.3 0.1 copy.8
  8.4 0.2 reduce-window.16
  8.6 0.1 add_reduce_fusion.1
  8.7 1.1 convolution_convert_fusion.2
  9.8 1.1 convolution_convert_fusion.1
  10.8 0.1 broadcast_in_dim.29
  11.0 0.1 broadcast_in_dim.28
  11.1 2.0 pad_maximum_fusion
  13.1 0.0 copy-start.1
  13.1 10.5 %all-to-all-start = ((bf16[32,96,512]{2,1,0:T(8,128)(2,1)}), bf16[32,96,512]{2,1,0:T(8,128)(2,1)}, u32[]{:S(2)}, u32[]{:S(2)}) async-start(bf16[32,96,512]{2,1,0:T(8,128)(2,1)} %pad_maximum_fusion), calls=%async_computation | async-start | bytes 6291456 | tf_op jit(solution)/shard_map/all_to_all | solution.py:48
  23.7 0.0 copy-done.1
  23.7 0.6 fusion.18
  24.3 0.6 fusion.15
  24.8 2.0 pad_maximum_fusion.1
  26.8 67.8 %all-to-all-done = bf16[32,96,512]{2,1,0:T(8,128)(2,1)} async-done(((bf16[32,96,512]{2,1,0:T(8,128)(2,1)}), bf16[32,96,512]{2,1,0:T(8,128)(2,1)}, u32[]{:S(2)}, u32[]{:S(2)}) %all-to-all-start) | async-done | bytes 3145760 | tf_op jit(solution)/shard_map/all_to_all | solution.py:48
  94.6 6.8 %all-to-all-start.2 = ((bf16[32,96,512]{2,1,0:T(8,128)(2,1)}), bf16[32,96,512]{2,1,0:T(8,128)(2,1)}, u32[]{:S(2)}, u32[]{:S(2)}) async-start(bf16[32,96,512]{2,1,0:T(8,128)(2,1)} %pad_maximum_fusion.1), calls=%async_computation.2 | async-start | bytes 6291456 | tf_op jit(solution)/shard_map/all_to_all | solution.py:47
  101.4 0.0 copy-done
  101.4 5.4 %convolution_convert_fusion = bf16[3072,512]{1,0:T(8,128)(2,1)} fusion(bf16[3072,512]{1,0:T(8,128)(2,1)} %bitcast.3, bf16[512,512]{1,0:T(8,128)(2,1)S(1)} %copy-done), kind=kOutput, calls=%fused_computation | convolution fusion | flops 1612185600 | bytes 6815744 | tf_op jit(solution)/shard_map/dot_general | solution.py:52
  106.9 65.5 %all-to-all-done.2 = bf16[32,96,512]{2,1,0:T(8,128)(2,1)} async-done(((bf16[32,96,512]{2,1,0:T(8,128)(2,1)}), bf16[32,96,512]{2,1,0:T(8,128)(2,1)}, u32[]{:S(2)}, u32[]{:S(2)}) %all-to-all-start.2) | async-done | bytes 3145760 | tf_op jit(solution)/shard_map/all_to_all | solution.py:47
  172.4 6.8 %all-to-all-start.1 = ((bf16[32,96,512]{2,1,0:T(8,128)(2,1)}), bf16[32,96,512]{2,1,0:T(8,128)(2,1)}, u32[]{:S(2)}, u32[]{:S(2)}) async-start(bf16[32,96,512]{2,1,0:T(8,128)(2,1)} %bitcast.44), calls=%async_computation.1 | async-start | bytes 6291456 | tf_op jit(solution)/shard_map/all_to_all | solution.py:55
  179.2 0.0 reduce-scatter.2.cloned.1.call-start
  179.2 5.6 %convolution_bitcast_fusion = f32[512,512]{1,0:T(8,128)} fusion(bf16[32,96,512]{2,1,0:T(8,128)(2,1)} %all-to-all-done.2, bf16[32,96,512]{2,1,0:T(8,128)(2,1)} %all-to-all-done), kind=kOutput, calls=%fused_computation.17 | convolution fusion | flops 1610612736 | bytes 7340032 | tf_op jit(solution)/shard_map/dot_general | solution.py:72
  184.9 0.0 reduce-scatter.2.cloned.1.call-update
  184.9 129.4 %reduce-scatter.2.cloned.1.call-done = f32[32,512]{1,0:T(8,128)} async-done(((f32[512,512]{1,0:T(8,128)}), f32[32,512]{1,0:T(8,128)}) %reduce-scatter.2.cloned.1.call-update) | async-done | bytes 65552 | tf_op jit(solution)/shard_map/reduce_scatter | solution.py:71
  314.2 1.5 broadcast_multiply_fusion
  315.7 0.0 all-to-all-done.1
  315.7 2.2 fusion.13
  317.9 3.5 %add_convert_fusion = bf16[128,16,512]{2,0,1:T(8,128)(2,1)} fusion(f32[128,16,512]{2,0,1:T(8,128)S(1)} %fusion.13, bf16[32,96,512]{2,1,0:T(8,128)(2,1)} %all-to-all-done.1, f32[128]{0:T(128)S(1)} %add_reduce_fusion, pred[128]{0:T(512)(128)(4,1)S(1)} %get-tuple-element.5), kind=kOutput, calls=%fused_computation.1 | convolution fusion | flops 203472896 | bytes 7864960 | tf_op jit(solution)/shard_map/ct,hcs->ths/dot_general | solution.py:66
  321.4 3.0 copy.10
  324.4 2.9 copy.11
Async XLA Ops:
  7.2 94.3 %copy-start = (bf16[512,512]{1,0:T(8,128)(2,1)S(1)}, bf16[512,512]{1,0:T(8,128)(2,1)}, u32[]{:S(2)}) copy-start(bf16[512,512]{1,0:T(8,128)(2,1)} %param.7) | copy-start | bytes 1572868
  13.1 10.6 %copy-start.1 = (bf16[128,8192]{1,0:T(8,128)(2,1)S(1)}, bf16[128,8192]{1,0:T(8,128)(2,1)}, u32[]{:S(2)}) copy-start(bf16[128,8192]{1,0:T(8,128)(2,1)} %param.4) | copy-start | bytes 6291460
  13.1 81.5 %all-to-all-start = ((bf16[32,96,512]{2,1,0:T(8,128)(2,1)}), bf16[32,96,512]{2,1,0:T(8,128)(2,1)}, u32[]{:S(2)}, u32[]{:S(2)}) async-start(bf16[32,96,512]{2,1,0:T(8,128)(2,1)} %pad_maximum_fusion), calls=%async_computation | async-start | bytes 6291456 | tf_op jit(solution)/shard_map/all_to_all | solution.py:48
  94.6 77.8 %all-to-all-start.2 = ((bf16[32,96,512]{2,1,0:T(8,128)(2,1)}), bf16[32,96,512]{2,1,0:T(8,128)(2,1)}, u32[]{:S(2)}, u32[]{:S(2)}) async-start(bf16[32,96,512]{2,1,0:T(8,128)(2,1)} %pad_maximum_fusion.1), calls=%async_computation.2 | async-start | bytes 6291456 | tf_op jit(solution)/shard_map/all_to_all | solution.py:47
  172.4 143.3 %all-to-all-start.1 = ((bf16[32,96,512]{2,1,0:T(8,128)(2,1)}), bf16[32,96,512]{2,1,0:T(8,128)(2,1)}, u32[]{:S(2)}, u32[]{:S(2)}) async-start(bf16[32,96,512]{2,1,0:T(8,128)(2,1)} %bitcast.44), calls=%async_computation.1 | async-start | bytes 6291456 | tf_op jit(solution)/shard_map/all_to_all | solution.py:55
  179.2 135.1 %reduce-scatter.2.cloned.1.call-start = ((), (), s32[]{:S(2)}) async-start(), calls=%async_computation.4 | async-start | bytes 1114112 | tf_op jit(solution)/shard_map/reduce_scatter | solution.py:71
Sparse Core Ops, SparseCore 0:
  185.0 129.1 reduce-scatter.1
where the time goes:
time: 335 us; the launch traced here: 334 us
  waiting for transfers between devices  263 us (79%)
  starting transfers between devices  24.2 us (7%)
  matrix products  20 us (6%)
  between operations  14.1 us (4%)
  other arithmetic  6.69 us (2%)
  local copies, waits for them, and re-layouts  6.45 us (2%)
    reduce_scatter x1, waiting for transfers between devices, body(): lax.psum_scatter(lax.dot_general(input_rows, output_rows, contract_rows,...  129 us
    all_to_all x1, waiting for transfers between devices, body(): lax.all_to_all(grads_send, 'mod', split_axis=0, concat_axis=0, tiled=True)  67.8 us
    all_to_all x1, waiting for transfers between devices, body(): lax.all_to_all(states_send, 'mod', split_axis=0, concat_axis=0, tiled=True)  65.5 us
    all_to_all x1, starting transfers between devices, body(): lax.all_to_all(grads_send, 'mod', split_axis=0, concat_axis=0, tiled=True)  10.5 us
    all_to_all x1, starting transfers between devices, body(): lax.all_to_all(states_send, 'mod', split_axis=0, concat_axis=0, tiled=True)  6.8 us
    all_to_all x1, starting transfers between devices, body(): lax.all_to_all(partial_dx.reshape(devices_mod, capacity, slice_width), 'm...  6.79 us
  transfers between devices with their start and end apart: 4, of which 3 were waited for; matrix products, arithmetic and copies ran while one was open for 5% of the time, Pallas kernels for 0%

commit v1 on v0

v1 whole, which is shorter than its diff:
```python
import functools

import jax
import jax.numpy as jnp
from jax import lax
from jax.experimental import pallas as pl
from jax.experimental.pallas import tpu as pltpu
from jax.sharding import PartitionSpec as P

MESH = pl.DeviceIdType.MESH
F32, BF16 = jnp.float32, jnp.bfloat16
ROWS, WIDTH, KV = 128, 8192, 512
HALF, QUARTER = ROWS // 2, ROWS // 4
GROUP = 8 * ROWS
ZL, ZH, NZ = 4, 4, 16

DIRS = (
    (1, 0, 0, HALF, 128),
    (-1, 0, HALF, HALF, 192),
    (0, 1, 0, HALF, 256),
    (0, -1, HALF, HALF, 320),
    (1, 1, 0, QUARTER, 384),
    (1, -1, QUARTER, QUARTER, 416),
    (-1, 1, 2 * QUARTER, QUARTER, 448),
    (-1, -1, 3 * QUARTER, QUARTER, 480),
)
ITEMS = ((0, 0, 1, 0, ROWS, 512, 1),) + tuple(
    (dx, dy, dc, row, rows, dc * 512 + slot, abs(dx) * 4 + abs(dy) * 2 + dc)
    for dx, dy, row, rows, slot in DIRS
    for dc in (0, 1)
)


def kernel(
    x_ref, k_ref, t_ref, w_ref, dx_ref, dw_ref,
    xs, xr, kr, k2, wr, part, down, up, dxs, dxr, last, total,
    stage_sem, x_send, x_recv, k_send, k_recv, w_send, w_recv, d_send, d_recv,
    c_send, c_recv, l_send, l_recv, local_sem, out_sem,
):
    dp, mod = lax.axis_index("dp"), lax.axis_index("mod")
    y, zh = lax.div(dp, 4), lax.rem(dp, 4)
    x, zl, c = lax.div(mod, 8), lax.rem(lax.div(mod, 2), 4), lax.rem(mod, 2)
    z = zh * 4 + zl
    px, py, jy = lax.rem(x, 2), lax.rem(y, 2), lax.div(y, 2)

    def device(dx, dy, dz, dc):
        xx, yy = lax.rem(x + dx + 4, 4), lax.rem(y + dy + 4, 4)
        zz, cc = lax.rem(z + dz + NZ, NZ), lax.rem(c + dc, 2)
        return (yy * 4 + lax.div(zz, 4), xx * 8 + lax.rem(zz, 4) * 2 + cc)

    def column(rel, l, j):
        xx, yy = lax.rem(px + rel // 4, 2), lax.rem(py + (rel // 2) % 2, 2)
        cc = lax.rem(c + rel % 2, 2)
        return pl.multiple_of(xx * 4096 + l * 1024 + cc * 512 + yy * 128 + j * 256, 128)

    def remote(src, dst, send, recv, to):
        return pltpu.make_async_remote_copy(
            src_ref=src, dst_ref=dst, send_sem=send, recv_sem=recv,
            device_id=to, device_id_type=MESH,
        )

    for rel in (4, 5, 2, 3, 6, 7, 1, 0):
        for l in range(ZL):
            for j in range(2):
                lanes = pl.ds(j * 128, 128)
                dst = xr.at[l, pl.ds(0, ROWS), lanes] if rel == 0 else xs.at[rel - 1, l, :, lanes]
                pltpu.make_async_copy(
                    x_ref.at[:, pl.ds(column(rel, l, j), 128)], dst, stage_sem.at[rel]
                ).start()
    kr[0:ROWS, 0:KV] = k_ref[...]
    kr[0:ROWS, KV:] = jnp.broadcast_to(t_ref[...].astype(F32), (ROWS, 128)).astype(BF16)

    barrier = pltpu.get_barrier_semaphore()
    greeted = [(dx, dy, 0, dc) for dx, dy, dc, *_ in ITEMS]
    greeted += [(0, 0, 1, 0), (0, 0, -1, 0), (0, 0, 2, 0), (0, 0, -2, 0)]
    greeted += [(2, 0, 0, 0), (0, 2, 0, 0), (2, 2, 0, 0)]
    for offsets in greeted:
        pl.semaphore_signal(barrier, inc=1, device_id=device(*offsets), device_id_type=MESH)
    pl.semaphore_wait(barrier, len(greeted))

    k_copies = []
    for i, (dx, dy, row, rows, slot) in enumerate(DIRS):
        copy = remote(
            kr.at[pl.ds(row, rows)], kr.at[pl.ds(slot, rows)], k_send.at[i], k_recv.at[i], device(dx, dy, 0, 0)
        )
        copy.start()
        k_copies.append(copy)
    k_own = remote(
        kr.at[pl.ds(0, ROWS)], kr.at[pl.ds(512, ROWS)], k_send.at[8], k_recv.at[8], device(0, 0, 0, 1)
    )
    k_own.start()
    w_copies = []
    for i, (dz, j) in enumerate(((1, 0), (1, 1), (-1, 0), (-1, 1), (2, 0), (-2, 1))):
        rows = w_ref.at[pl.ds(pl.multiple_of((py + 2 * j) * 128, 128), 128)]
        copy = remote(rows, wr.at[0, zl, j], w_send.at[i], w_recv.at[i], device(0, 0, dz, 0))
        copy.start()
        w_copies.append((copy, i, lax.rem(zl + NZ - dz, 4), j))
    for j in range(2):
        rows = w_ref.at[pl.ds(pl.multiple_of((py + 2 * j) * 128, 128), 128)]
        pltpu.make_async_copy(rows, wr.at[0, zl, j], local_sem.at[j]).start()
    staged = set()
    x_copies = []
    for i in list(range(1, len(ITEMS))) + [0]:
        dx, dy, dc, row, rows, slot, rel = ITEMS[i]
        if rel not in staged:
            staged.add(rel)
            pltpu.make_async_copy(xs.at[rel - 1], xs.at[rel - 1], stage_sem.at[rel]).wait()
        copy = remote(
            xs.at[rel - 1, :, pl.ds(row, rows)], xr.at[:, pl.ds(slot, rows)],
            x_send.at[i], x_recv.at[i], device(dx, dy, 0, dc),
        )
        copy.start()
        x_copies.append(copy)
    mine = xr.at[:, pl.ds(0, ROWS)]
    pltpu.make_async_copy(mine, mine, stage_sem.at[0]).wait()

    for copy in k_copies:
        copy.wait_recv()
    relay = remote(
        kr.at[pl.ds(128, 384)], kr.at[pl.ds(640, 384)], k_send.at[9], k_recv.at[9], device(0, 0, 0, 1)
    )
    relay.start()
    k_own.wait_recv()
    relay.wait_recv()
    own_kind = lax.div(x, 2).astype(F32)
    for i in range(8):
        rows = pl.ds(i * 128, 128)
        kind = kr[rows, KV:].astype(F32)
        mask = 1.0 - jnp.abs(kind - own_kind)
        mask = jnp.concatenate([mask] * 4, 1)
        values = kr[rows, 0:KV].astype(F32)
        k2[rows, 0:KV] = (values * mask).astype(BF16)
        k2[rows, KV:] = (values * (1.0 - mask)).astype(BF16)

    for copy, i, l, j in w_copies:
        here = wr.at[0, l, j]
        pltpu.make_async_copy(here, here, w_recv.at[i]).wait()
    for j in range(2):
        here = wr.at[0, zl, j]
        pltpu.make_async_copy(here, here, local_sem.at[j]).wait()
    wx_copies = []
    for l in range(ZL):
        copy = remote(
            wr.at[0, l, jy], wr.at[1, l, jy], w_send.at[6 + l], w_recv.at[6 + l], device(2, 0, 0, 0)
        )
        copy.start()
        wx_copies.append(copy)

    for copy in x_copies:
        copy.wait_recv()
    for l in range(ZL):
        for half in range(2):
            lanes = pl.ds(half * KV, KV)
            value = lax.dot_general(
                xr[l], k2[:, lanes], (((0,), (0,)), ((), ())), preferred_element_type=F32
            )
            part[l, :, :, :, lanes] = value.reshape(2, ZH, 32, KV)

    def chunk(target):
        target = lax.rem(target + NZ, NZ)
        return lax.rem(target, 4), lax.div(target, 4)

    chains = []

    def chain(step):
        for at, (buffer, dz, target, count) in enumerate(
            ((down, -1, z + 8 + step, 8), (up, 1, z + 7 - step, 7))
        ):
            if step >= count:
                continue
            l, h = chunk(target)
            if step == 0:
                src = part.at[l, :, h]
            else:
                chains[2 * (step - 1) + at].wait_recv()
                src = buffer.at[step - 1]
                src[...] = src[...] + part[l, :, h]
            i = at * 8 + step
            copy = remote(src, buffer.at[step], c_send.at[i], c_recv.at[i], device(0, 0, dz, 0))
            copy.start()
            chains.append(copy)

    wy_copies = []

    def weights_y():
        for l in range(ZL):
            wx_copies[l].wait_recv()
            copy = remote(
                wr.at[1, l, jy], wr.at[1, l, jy], w_send.at[10 + l], w_recv.at[10 + l], device(0, 2, 0, 0)
            )
            copy.start()
            wy_copies.append(copy)

    d_copies = []

    def state_grad(l):
        here = wr.at[1, l, 1 - jy]
        pltpu.make_async_copy(here, here, w_recv.at[10 + l]).wait()
        own, other = wr[0, l].reshape(256, KV), wr[1, l].reshape(256, KV)
        for half in range(2):
            rows = pl.ds(half * 512, 512)
            dims = (((1,), (1,)), ((), ()))
            value = lax.dot_general(k2[rows, 0:KV], own, dims, preferred_element_type=F32)
            value += lax.dot_general(k2[rows, KV:], other, dims, preferred_element_type=F32)
            dxs[l, rows] = value.astype(BF16)
        for i, (dx, dy, dc, row, rows, slot, rel) in enumerate(ITEMS):
            copy = remote(
                dxs.at[l, pl.ds(slot, rows)], dxr.at[rel - 1, l, pl.ds(row, rows)],
                d_send.at[l, i], d_recv.at[l, i], device(-dx, -dy, 0, dc),
            )
            copy.start()
            d_copies.append(copy)
        for j in range(2):
            lanes = pl.ds(j * 128, 128)
            pltpu.make_async_copy(
                dxs.at[l, pl.ds(0, ROWS), lanes], dx_ref.at[:, pl.ds(column(0, l, j), 128)], out_sem.at[0]
            ).start()

    chain(0)
    weights_y()
    chain(1)
    chain(2)
    for l in range(ZL):
        state_grad(l)
        chain(3 + l)
    chain(7)

    chains[15 - 1].wait_recv()
    chains[13].wait_recv()
    total[...] = part[zl, :, zh] + down[7] + up[6]
    l_copies = []
    for i, (dx, dy, j, first) in enumerate(
        ((2, 0, jy, KV), (0, 2, 1 - jy, 0), (2, 2, 1 - jy, KV))
    ):
        copy = remote(
            total.at[j, :, pl.ds(first, KV)], last.at[i], l_send.at[i], l_recv.at[i], device(dx, dy, 0, 0)
        )
        copy.start()
        l_copies.append(copy)

    for copy in d_copies:
        copy.wait_recv()
    for rel in range(1, 8):
        for l in range(ZL):
            for j in range(2):
                pltpu.make_async_copy(
                    dxr.at[rel - 1, l, :, pl.ds(j * 128, 128)],
                    dx_ref.at[:, pl.ds(column(rel, l, j), 128)],
                    out_sem.at[0],
                ).start()
    for copy in l_copies:
        copy.wait_recv()
    dw_ref[...] = (total[jy, :, 0:KV] + last[0] + last[1] + last[2]) * (1.0 / 256.0)

    pltpu.make_async_copy(dx_ref, dx_ref, out_sem.at[0]).wait()
    for copy in k_copies + [k_own, relay] + x_copies + wx_copies + wy_copies + chains + d_copies + l_copies:
        copy.wait_send()
    for copy, *_ in w_copies:
        copy.wait_send()


def body(normed_states, kv_cotangent, token_types, kv_weight):
    any_spec, vmem = pl.BlockSpec(memory_space=pl.ANY), pl.BlockSpec(memory_space=pltpu.VMEM)
    dma = pltpu.SemaphoreType.DMA
    return pl.pallas_call(
        kernel,
        out_shape=(
            jax.ShapeDtypeStruct((ROWS, WIDTH), BF16),
            jax.ShapeDtypeStruct((32, KV), F32),
        ),
        in_specs=[any_spec, vmem, vmem, vmem],
        out_specs=(any_spec, vmem),
        scratch_shapes=[
            pltpu.VMEM((7, ZL, ROWS, 256), BF16),
            pltpu.VMEM((ZL, GROUP, 256), BF16),
            pltpu.VMEM((GROUP, KV + 128), BF16),
            pltpu.VMEM((GROUP, 2 * KV), BF16),
            pltpu.VMEM((2, ZL, 2, 128, KV), BF16),
            pltpu.VMEM((ZL, 2, ZH, 32, 2 * KV), F32),
            pltpu.VMEM((8, 2, 32, 2 * KV), F32),
            pltpu.VMEM((7, 2, 32, 2 * KV), F32),
            pltpu.VMEM((ZL, GROUP, 256), BF16),
            pltpu.VMEM((7, ZL, ROWS, 256), BF16),
            pltpu.VMEM((3, 32, KV), F32),
            pltpu.VMEM((2, 32, 2 * KV), F32),
            dma((8,)),
            dma((len(ITEMS),)),
            dma((len(ITEMS),)),
            dma((10,)),
            dma((10,)),
            dma((14,)),
            dma((14,)),
            dma((ZL, len(ITEMS))),
            dma((ZL, len(ITEMS))),
            dma((16,)),
            dma((16,)),
            dma((3,)),
            dma((3,)),
            dma((2,)),
            dma((1,)),
        ],
        compiler_params=pltpu.CompilerParams(
            collective_id=0, has_side_effects=True, vmem_limit_bytes=48 * 2**20
        ),
        cost_estimate=pl.CostEstimate(flops=2**32, bytes_accessed=5 * 2**20, transcendentals=0),
        name="exchange",
    )(normed_states, kv_cotangent, token_types, kv_weight)


def solution(mesh):
    in_specs = (
        P(("dp", "mod"), None),
        P(("dp", "mod"), None),
        P(("dp", "mod"), None),
        P("mod", None),
    )
    out_specs = (P(("dp", "mod"), None), P(("mod", "dp"), None))
    return jax.shard_map(body, mesh=mesh, in_specs=in_specs, out_specs=out_specs, check_vma=False)
```

time: 335 us -> 109 us (0.33)
  waiting for transfers between devices: 263 us -> 0 us
  Pallas kernels: 0 us -> 101 us
  starting transfers between devices: 24.2 us -> 0 us
  matrix products: 20 us -> 0 us
  between operations: 14.1 us -> 0.65 us
  other arithmetic: 6.69 us -> 0 us
    all_to_all x3 -> x0, waiting for transfers between devices: 133 us -> none  [the longest x1 67.8 us: body(): lax.all_to_all(grads_send, 'mod', split_axis=0, concat_axis=0, tiled=True)]
    reduce_scatter x1 -> x0, waiting for transfers between devices: 129 us -> none  [body(): lax.psum_scatter(lax.dot_general(input_rows, output_rows, contract_rows,...]
    pallas_call x0 -> x1, Pallas kernels: none -> 101 us  [body(): pl.pallas_call(kernel, out_shape=(jax.ShapeDtypeStruct((ROWS, WIDTH), BF1...]
    all_to_all x3 -> x0, starting transfers between devices: 24.1 us -> none  [the longest x1 10.5 us: body(): lax.all_to_all(grads_send, 'mod', split_axis=0, concat_axis=0, tiled=True)]
    dot_general x8 -> x0, matrix products: 20 us -> none  [the longest x1 5.63 us: body(): lax.dot_general(input_rows, output_rows, contract_rows, preferred_element...]
    concatenate x2 -> x0, other arithmetic: 3.95 us -> none  [the longest x1 1.97 us: body(): grads_send = jnp.concatenate(grad_parts, 0)]
  transfers between devices with their start and end apart: 4 -> 0, of which waited for: 3 -> 0; matrix products, arithmetic and copies ran while one was open for 5% -> 0% of each run, Pallas kernels for 0% -> 0%
where the time goes in v1:
time: 109 us; the launch traced here: 108 us
  Pallas kernels  101 us (93%)
  local copies, waits for them, and re-layouts  6.24 us (6%)
    pallas_call x1, Pallas kernels, body(): pl.pallas_call(kernel, out_shape=(jax.ShapeDtypeStruct((ROWS, WIDTH), BF1...  101 us
    unnamed x9, local copies, waits for them, and re-layouts  6.24 us

profile of v1, /device:TPU:6, one launch (start us, length us, event | category | flops | bytes accessed | tf_op | source)
XLA Modules:
  0.0 108.4 jit_solution(12008259468891072232)
XLA Ops:
  0.6 0.8 copy.6.t_ref
  1.4 0.0 copy-start
  1.4 1.6 %copy-done = bf16[128,8192]{1,0:T(8,128)(2,1)S(1)} copy-done((bf16[128,8192]{1,0:T(8,128)(2,1)S(1)}, bf16[128,8192]{1,0:T(8,128)(2,1)}, u32[]{:S(2)}) %copy-start) | copy-done | bytes 2097176
  3.0 0.0 copy-start.1
  3.0 1.0 copy-done.1
  4.0 0.0 copy-start.2
  4.0 0.9 copy-done.2
  4.9 101.5 %exchange.1 = (bf16[128,8192]{1,0:T(8,128)(2,1)S(1)}, f32[32,512]{1,0:T(8,128)S(1)}) custom-call(bf16[128,8192]{1,0:T(8,128)(2,1)S(1)} %copy-done, bf16[128,512]{1,0:T(8,128)(2,1)S(1)} %copy-done.2, s32[128,1]{1,0:T(8,128)S(1)} %copy.6.t_ref, bf16[512,512]{1,0:T(8,128)(2,1)S(1)} %copy-done.1), custom_call_target="tpu_custom_call" | custom-call | flops 4294967296 | bytes 5242880 | tf_op jit(solution)/shard_map/exchange/pallas_call | solution.py:265
  106.4 1.3 %copy.9 = bf16[128,8192]{1,0:T(8,128)(2,1)} copy(bf16[128,8192]{1,0:T(8,128)(2,1)S(1)} %get-tuple-element.4) | data formatting | bytes 4194304
  107.8 0.6 copy.10
Async XLA Ops:
  1.4 1.6 %copy-start = (bf16[128,8192]{1,0:T(8,128)(2,1)S(1)}, bf16[128,8192]{1,0:T(8,128)(2,1)}, u32[]{:S(2)}) copy-start(bf16[128,8192]{1,0:T(8,128)(2,1)} %x_ref.1) | copy-start | bytes 6291460
  3.0 1.0 copy-start.1
  4.0 0.9 copy-start.2

commit v2 on v1

v2 whole, which is shorter than its diff:
```python
import jax
import jax.numpy as jnp
from jax import lax
from jax.experimental import pallas as pl
from jax.experimental.pallas import tpu as pltpu
from jax.sharding import PartitionSpec as P

MESH = pl.DeviceIdType.MESH
F32, BF16, I16, I32 = jnp.float32, jnp.bfloat16, jnp.int16, jnp.int32
ROWS, WIDTH, KV = 128, 8192, 512
HALF, QUARTER = ROWS // 2, ROWS // 4
GROUP = 8 * ROWS
ZL, ZH, NZ = 4, 4, 16
UNIT = 16
TOP = 32767.0

DIRS = (
    (1, 0, 0, HALF, 128),
    (-1, 0, HALF, HALF, 192),
    (0, 1, 0, HALF, 256),
    (0, -1, HALF, HALF, 320),
    (1, 1, 0, QUARTER, 384),
    (1, -1, QUARTER, QUARTER, 416),
    (-1, 1, 2 * QUARTER, QUARTER, 448),
    (-1, -1, 3 * QUARTER, QUARTER, 480),
)
ITEMS = tuple(
    (dx, dy, dc, row, rows, dc * 512 + slot, abs(dx) * 4 + abs(dy) * 2 + dc)
    for dx, dy, row, rows, slot in DIRS
    for dc in (0, 1)
) + ((0, 0, 1, 0, ROWS, 512, 1),)
ALONG_Z = ((1, 0, 128, 1), (-1, 0, 128, 2), (2, 0, 64, 3), (-2, 64, 64, 3))


def kernel(
    x_ref, k_ref, t_ref, w_ref, dx_ref, dw_ref,
    xs, xr, kr, k2, kinds, wr, part, sums, units, dxs, dxr, last, total,
    stage_sem, x_send, x_recv, k_send, k_recv, w_send, w_recv, d_send, d_recv,
    c_send, c_recv, l_send, l_recv, local_sem, out_sem,
):
    dp, mod = lax.axis_index("dp"), lax.axis_index("mod")
    y, zh = lax.div(dp, 4), lax.rem(dp, 4)
    x, zl, c = lax.div(mod, 8), lax.rem(lax.div(mod, 2), 4), lax.rem(mod, 2)
    z = zh * 4 + zl
    px, py, jy = lax.rem(x, 2), lax.rem(y, 2), lax.div(y, 2)
    jn = 1 - jy

    def device(dx, dy, dz, dc):
        xx, yy = lax.rem(x + dx + 4, 4), lax.rem(y + dy + 4, 4)
        zz, cc = lax.rem(z + dz + NZ, NZ), lax.rem(c + dc, 2)
        return (yy * 4 + lax.div(zz, 4), xx * 8 + lax.rem(zz, 4) * 2 + cc)

    def column(rel, l, j):
        xx, yy = lax.rem(px + rel // 4, 2), lax.rem(py + (rel // 2) % 2, 2)
        cc = lax.rem(c + rel % 2, 2)
        return pl.multiple_of(xx * 4096 + l * 1024 + cc * 512 + yy * 128 + j * 256, 128)

    def remote(src, dst, send, recv, to):
        return pltpu.make_async_remote_copy(
            src_ref=src, dst_ref=dst, send_sem=send, recv_sem=recv,
            device_id=to, device_id_type=MESH,
        )

    def landed(ref, sem):
        pltpu.make_async_copy(ref, ref, sem).wait()

    barrier = pltpu.get_barrier_semaphore()
    greeted = [(dx, dy, 0, dc) for dx, dy, dc, *_ in ITEMS]
    greeted += [(0, 0, 1, 0), (0, 0, -1, 0), (0, 0, 2, 0), (0, 0, -2, 0)]
    greeted += [(2, 0, 0, 0), (0, 2, 0, 0), (2, 2, 0, 0)]
    for offsets in greeted:
        pl.semaphore_signal(barrier, inc=1, device_id=device(*offsets), device_id_type=MESH)

    k_in = pltpu.make_async_copy(k_ref, kr.at[pl.ds(0, ROWS), pl.ds(0, KV)], local_sem.at[0])
    k_in.start()
    t_in = pltpu.make_async_copy(t_ref, kinds, local_sem.at[1])
    t_in.start()
    for rel in (4, 5, 2, 3, 6, 7, 1):
        for l in range(ZL):
            for j in range(2):
                pltpu.make_async_copy(
                    x_ref.at[:, pl.ds(column(rel, l, j), 128)],
                    xs.at[rel - 1, j, :, pl.ds(l * 128, 128)],
                    stage_sem.at[rel],
                ).start()
    for o, j in enumerate((jn, jy)):
        for l in range(ZL):
            pltpu.make_async_copy(
                x_ref.at[:, pl.ds(column(0, l, j), 128)],
                xr.at[o, pl.ds(0, ROWS), pl.ds(l * 128, 128)],
                stage_sem.at[0],
            ).start()
    for r, j in enumerate((jy, jn)):
        rows = pl.ds(pl.multiple_of((py + 2 * j) * 128, 128), 128)
        pltpu.make_async_copy(w_ref.at[rows], wr.at[0, j, zl], local_sem.at[2 + r]).start()
    k_in.wait()
    t_in.wait()
    kr[0:ROWS, KV:] = jnp.broadcast_to(kinds[...].astype(F32), (ROWS, 128)).T.astype(BF16)

    pl.semaphore_wait(barrier, len(greeted))

    w_copies, d_copies, chains = [], [], {}
    blocks = [lax.rem(zl + 4 + d, 4) for d in (0, -1, 1, 2)]

    def w_along_z(r):
        j = (jy, jn, jy)[r]
        for i, (dz, row, rows, _) in enumerate(ALONG_Z):
            start = pl.multiple_of((py + 2 * j) * 128 + row, 64)
            dst = wr.at[r // 2, j, zl, pl.ds(row, rows)]
            copy = remote(
                dst if r == 2 else w_ref.at[pl.ds(start, rows)], dst,
                w_send.at[4 * r + i], w_recv.at[4 * r + i], device(0, 0, dz, 0),
            )
            copy.start()
            w_copies.append(copy)

    def w_arrived(r, q):
        j = (jy, jn, jy)[r]
        if q == 0 and r < 2:
            landed(wr.at[0, j, zl], local_sem.at[2 + r])
        for i, (_, row, rows, place) in enumerate(ALONG_Z):
            if place == q:
                landed(wr.at[r // 2, j, blocks[q], pl.ds(row, rows)], w_recv.at[4 * r + i])

    w_across = remote(
        w_ref.at[pl.ds(pl.multiple_of((py + 2 * jy) * 128, 128), 128)], wr.at[1, jy, zl],
        w_send.at[12], w_recv.at[12], device(2, 0, 0, 0),
    )

    def w_along_y(q):
        w_arrived(2, q)
        ref = wr.at[1, jy, blocks[q]]
        copy = remote(ref, ref, w_send.at[13 + q], w_recv.at[13 + q], device(0, 2, 0, 0))
        copy.start()
        w_copies.append(copy)

    def w_all(r):
        for q in range(4):
            w_arrived(r, q)
            if r == 1:
                landed(wr.at[1, jn, blocks[q]], w_recv.at[13 + q])

    k_copies = []
    for i, (dx, dy, row, rows, slot) in enumerate(DIRS):
        copy = remote(
            kr.at[pl.ds(row, rows)], kr.at[pl.ds(slot, rows)], k_send.at[i], k_recv.at[i], device(dx, dy, 0, 0)
        )
        copy.start()
        k_copies.append(copy)
    k_own = remote(
        kr.at[pl.ds(0, ROWS)], kr.at[pl.ds(512, ROWS)], k_send.at[8], k_recv.at[8], device(0, 0, 0, 1)
    )
    k_own.start()
    x_copies = ([], [])
    staged = set()
    for o in range(2):
        if o == 0:
            w_across.start()
            w_copies.append(w_across)
            w_along_z(0)
        for i, (dx, dy, dc, row, rows, slot, rel) in enumerate(ITEMS):
            if rel not in staged:
                staged.add(rel)
                landed(xs.at[rel - 1], stage_sem.at[rel])
            there = lax.div(lax.rem(y + dy + 4, 4), 2)
            copy = remote(
                xs.at[rel - 1, there if o else 1 - there, pl.ds(row, rows)],
                xr.at[o, pl.ds(slot, rows)],
                x_send.at[o, i], x_recv.at[o, i], device(dx, dy, 0, dc),
            )
            copy.start()
            x_copies[o].append(copy)
    landed(xr.at[:, pl.ds(0, ROWS)], stage_sem.at[0])

    w_across.wait_recv()
    w_along_z(2)
    w_along_z(1)
    for copy in k_copies:
        copy.wait_recv()
    relay = remote(
        kr.at[pl.ds(128, 384)], kr.at[pl.ds(640, 384)], k_send.at[9], k_recv.at[9], device(0, 0, 0, 1)
    )
    relay.start()
    k_own.wait_recv()
    own_kind = lax.div(x, 2).astype(F32)

    def masked(i):
        rows = pl.ds(i * 128, 128)
        mask = (1.0 - jnp.abs(kr[rows, KV:].astype(F32) - own_kind)).astype(BF16)
        values = kr[rows, 0:KV]
        own = values * jnp.concatenate([mask] * 4, 1)
        k2[rows, 0:KV] = own
        k2[rows, KV:] = values - own

    for i in range(5):
        masked(i)
    relay.wait_recv()
    for i in range(5, 8):
        masked(i)

    def partial(o):
        for copy in x_copies[o]:
            copy.wait_recv()
        for half in range(2):
            lanes = pl.ds(half * KV, KV)
            value = lax.dot_general(
                xr[o], k2[:, lanes], (((0,), (0,)), ((), ())), preferred_element_type=F32
            )
            part[o, :, :, :, lanes] = value.reshape(ZL, ZH, 32, KV)

    def state_grad(r, block):
        j = (jy, jn)[r]
        rows = pl.ds(block * 256, 256)
        dims = (((1,), (1,)), ((), ()))
        own, other = wr[0, j].reshape(512, KV), wr[1, j].reshape(512, KV)
        value = lax.dot_general(k2[rows, 0:KV], own, dims, preferred_element_type=F32)
        value += lax.dot_general(k2[rows, KV:], other, dims, preferred_element_type=F32)
        dxs[j, rows] = value.astype(BF16)
        for i, (dx, dy, dc, row, n, slot, rel) in enumerate(ITEMS):
            if slot // 256 != block:
                continue
            copy = remote(
                dxs.at[j, pl.ds(slot, n)], dxr.at[rel - 1, j, pl.ds(row, n)],
                d_send.at[r, i], d_recv.at[r, i], device(-dx, -dy, 0, dc),
            )
            copy.start()
            d_copies.append(copy)

    def chunk(target):
        target = lax.rem(target + NZ, NZ)
        return lax.rem(target, 4), lax.div(target, 4)

    def chain(step, o, half):
        rows = pl.ds(half * UNIT, UNIT)
        for at, (dz, target, count) in enumerate(((-1, z + 8 + step, 8), (1, z + 7 - step, 7))):
            if step >= count:
                continue
            if step > 0:
                for copy in chains[step - 1, o, half, at]:
                    copy.wait_recv()
            l, h = chunk(target)
            codes, scale = sums.at[at, step, o, half], units.at[at, step, o, half]
            value = part[o, l, h, rows]
            if step > 0:
                value += codes[...].astype(F32) * scale[0:1, 0:1]
            top = jnp.maximum(jnp.max(jnp.abs(value), keepdims=True), 1e-30)
            codes[...] = jnp.round(value * (TOP / top)).astype(I32).astype(I16)
            scale[...] = jnp.broadcast_to(top * (1.0 / TOP), (8, 128))
            to, copies = device(0, 0, dz, 0), []
            for i, ref in enumerate((units, sums)):
                copy = remote(
                    ref.at[at, step, o, half], ref.at[at, step + 1, o, half],
                    c_send.at[at, step, o, half, i], c_recv.at[at, step, o, half, i], to,
                )
                copy.start()
                copies.append(copy)
            chains[step, o, half, at] = copies

    partial(0)
    for half in range(2):
        chain(0, 0, half)
    partial(1)
    for half in range(2):
        chain(0, 1, half)
    for q in range(4):
        w_along_y(q)

    background = {
        (1, 0): lambda: (w_all(0), state_grad(0, 0)),
        (1, 2): lambda: state_grad(0, 1),
        (2, 0): lambda: state_grad(0, 2),
        (2, 2): lambda: state_grad(0, 3),
        (4, 0): lambda: (w_all(1), state_grad(1, 0)),
        (4, 2): lambda: state_grad(1, 1),
        (5, 0): lambda: state_grad(1, 2),
        (5, 2): lambda: state_grad(1, 3),
    }
    for step in range(1, 8):
        for unit in range(4):
            chain(step, unit // 2, unit % 2)
            if (step, unit) in background:
                background[step, unit]()

    l_copies = []
    for o in range(2):
        for half in range(2):
            rows = pl.ds(half * UNIT, UNIT)
            value = part[o, zl, zh, rows]
            for at, count in ((0, 8), (1, 7)):
                for copy in chains[count - 1, o, half, at]:
                    copy.wait_recv()
                value += sums[at, count, o, half].astype(F32) * units[at, count, o, half, 0:1, 0:1]
            total[o, rows] = value
        for i, dx, dy, first in (((0, 2, 2, KV), (1, 0, 2, 0)), ((2, 2, 0, KV),))[o]:
            copy = remote(
                total.at[o, :, pl.ds(first, KV)], last.at[i], l_send.at[i], l_recv.at[i], device(dx, dy, 0, 0)
            )
            copy.start()
            l_copies.append(copy)

    for copy in d_copies:
        copy.wait_recv()
    for rel in range(8):
        for l in range(ZL):
            for j in range(2):
                lanes = pl.ds(l * 128, 128)
                src = dxs.at[j, pl.ds(0, ROWS), lanes] if rel == 0 else dxr.at[rel - 1, j, :, lanes]
                pltpu.make_async_copy(src, dx_ref.at[:, pl.ds(column(rel, l, j), 128)], out_sem.at[0]).start()
    for copy in l_copies:
        copy.wait_recv()
    dw_ref[...] = (total[1, :, 0:KV] + last[0] + last[1] + last[2]) * (1.0 / 256.0)

    landed(dx_ref, out_sem.at[0])
    for copy in k_copies + [k_own, relay] + x_copies[0] + x_copies[1] + w_copies:
        copy.wait_send()
    for copy in d_copies + l_copies:
        copy.wait_send()
    for copies in chains.values():
        for copy in copies:
            copy.wait_send()


def body(normed_states, kv_cotangent, token_types, kv_weight):
    any_spec, vmem = pl.BlockSpec(memory_space=pl.ANY), pl.BlockSpec(memory_space=pltpu.VMEM)
    dma = pltpu.SemaphoreType.DMA
    return pl.pallas_call(
        kernel,
        out_shape=(
            jax.ShapeDtypeStruct((ROWS, WIDTH), BF16),
            jax.ShapeDtypeStruct((32, KV), F32),
        ),
        in_specs=[any_spec] * 4,
        out_specs=(any_spec, vmem),
        scratch_shapes=[
            pltpu.VMEM((7, 2, ROWS, KV), BF16),
            pltpu.VMEM((2, GROUP, KV), BF16),
            pltpu.VMEM((GROUP, KV + 128), BF16),
            pltpu.VMEM((GROUP, 2 * KV), BF16),
            pltpu.VMEM((1, ROWS), I32),
            pltpu.VMEM((2, 2, ZL, 128, KV), BF16),
            pltpu.VMEM((2, ZL, ZH, 32, 2 * KV), F32),
            pltpu.VMEM((2, 9, 2, 2, UNIT, 2 * KV), I16),
            pltpu.VMEM((2, 9, 2, 2, 8, 128), F32),
            pltpu.VMEM((2, GROUP, KV), BF16),
            pltpu.VMEM((7, 2, ROWS, KV), BF16),
            pltpu.VMEM((3, 32, KV), F32),
            pltpu.VMEM((2, 32, 2 * KV), F32),
            dma((8,)),
            dma((2, len(ITEMS))),
            dma((2, len(ITEMS))),
            dma((10,)),
            dma((10,)),
            dma((17,)),
            dma((17,)),
            dma((2, len(ITEMS))),
            dma((2, len(ITEMS))),
            dma((2, 8, 2, 2, 2)),
            dma((2, 8, 2, 2, 2)),
            dma((3,)),
            dma((3,)),
            dma((4,)),
            dma((1,)),
        ],
        compiler_params=pltpu.CompilerParams(
            collective_id=0, has_side_effects=True, vmem_limit_bytes=60 * 2**20
        ),
        cost_estimate=pl.CostEstimate(flops=2**32, bytes_accessed=5 * 2**20, transcendentals=0),
        name="exchange",
    )(normed_states, kv_cotangent, token_types.reshape(1, ROWS), kv_weight)


def solution(mesh):
    in_specs = (
        P(("dp", "mod"), None),
        P(("dp", "mod"), None),
        P(("dp", "mod"), None),
        P("mod", None),
    )
    out_specs = (P(("dp", "mod"), None), P(("mod", "dp"), None))
    return jax.shard_map(body, mesh=mesh, in_specs=in_specs, out_specs=out_specs, check_vma=False)
```

time: 109 us -> 81.8 us (0.75)
  Pallas kernels: 101 us -> 76.3 us
  local copies, waits for them, and re-layouts: 6.24 us -> 3.76 us
    pallas_call x1, Pallas kernels: 101 us -> 76.3 us  [body(): pl.pallas_call(kernel, out_shape=(jax.ShapeDtypeStruct((ROWS, WIDTH), BF1...]
    unnamed x9 -> x4, local copies, waits for them, and re-layouts: 6.24 us -> 3.76 us
where the time goes in v2:
time: 81.8 us; the launch traced here: 80.7 us
  Pallas kernels  76.3 us (93%)
  local copies, waits for them, and re-layouts  3.76 us (5%)
    pallas_call x1, Pallas kernels, body(): pl.pallas_call(kernel, out_shape=(jax.ShapeDtypeStruct((ROWS, WIDTH), BF1...  76.3 us
    unnamed x4, local copies, waits for them, and re-layouts  3.76 us

profile of v2, /device:TPU:6, one launch (start us, length us, event | category | flops | bytes accessed | tf_op | source)
XLA Modules:
  0.0 80.7 jit_solution(14080328901378969815)
XLA Ops:
  0.6 76.3 %exchange.1 = (bf16[128,8192]{1,0:T(8,128)(2,1)}, f32[32,512]{1,0:T(8,128)}) custom-call(bf16[128,8192]{1,0:T(8,128)(2,1)} %x_ref.1, bf16[128,512]{1,0:T(8,128)(2,1)} %k_ref.1, s32[1,128]{1,0:T(1,128)} %bitcast.1, bf16[512,512]{1,0:T(8,128)(2,1)} %w_ref.1), custom_call_target="tpu_custom_call" | custom-call | flops 4294967296 | bytes 5242880 | tf_op jit(solution)/shard_map/exchange/pallas_call | solution.py:326
  76.9 0.0 copy-start
  76.9 3.1 %copy.8 = bf16[128,8192]{1,0:T(8,128)(2,1)} copy(bf16[128,8192]{1,0:T(8,128)(2,1)} %get-tuple-element.4) | data formatting | bytes 4194304
  80.0 0.0 copy-done
  80.1 0.6 copy.9
Async XLA Ops:
  76.9 3.1 %copy-start = (f32[32,512]{1,0:T(8,128)S(1)}, f32[32,512]{1,0:T(8,128)}, u32[]{:S(2)}) copy-start(f32[32,512]{1,0:T(8,128)} %get-tuple-element.5) | copy-start | bytes 196612

commit v3 on v2

--- a/solution.py
+++ b/solution.py
@@ -127,18 +127,19 @@
         w_send.at[12], w_recv.at[12], device(2, 0, 0, 0),
     )
 
-    def w_along_y(q):
-        w_arrived(2, q)
-        ref = wr.at[1, jy, blocks[q]]
-        copy = remote(ref, ref, w_send.at[13 + q], w_recv.at[13 + q], device(0, 2, 0, 0))
+    def w_other_half(q):
+        if q < 2:
+            w_arrived(1, q)
+            copy = remote(
+                wr.at[0, jn, blocks[q]], wr.at[1, jn, blocks[q]],
+                w_send.at[13 + q], w_recv.at[13 + q], device(2, 0, 0, 0),
+            )
+        else:
+            w_arrived(2, q)
+            ref = wr.at[1, jy, blocks[q]]
+            copy = remote(ref, ref, w_send.at[13 + q], w_recv.at[13 + q], device(0, 2, 0, 0))
         copy.start()
         w_copies.append(copy)
-
-    def w_all(r):
-        for q in range(4):
-            w_arrived(r, q)
-            if r == 1:
-                landed(wr.at[1, jn, blocks[q]], w_recv.at[13 + q])
 
     k_copies = []
     for i, (dx, dy, row, rows, slot) in enumerate(DIRS):
@@ -172,9 +173,6 @@
             x_copies[o].append(copy)
     landed(xr.at[:, pl.ds(0, ROWS)], stage_sem.at[0])
 
-    w_across.wait_recv()
-    w_along_z(2)
-    w_along_z(1)
     for copy in k_copies:
         copy.wait_recv()
     relay = remote(
@@ -197,6 +195,9 @@
     relay.wait_recv()
     for i in range(5, 8):
         masked(i)
+    w_across.wait_recv()
+    w_along_z(2)
+    w_along_z(1)
 
     def partial(o):
         for copy in x_copies[o]:
@@ -208,23 +209,42 @@
             )
             part[o, :, :, :, lanes] = value.reshape(ZL, ZH, 32, KV)
 
-    def state_grad(r, block):
-        j = (jy, jn)[r]
+    dims = (((1,), (1,)), ((), ()))
+
+    def send_back(n, j, first, last, lanes):
+        for i, (dx, dy, dc, row, rows, slot, rel) in enumerate(ITEMS):
+            if first <= slot < last:
+                copy = remote(
+                    dxs.at[j, pl.ds(slot, rows), lanes], dxr.at[rel - 1, j, pl.ds(row, rows), lanes],
+                    d_send.at[n, i], d_recv.at[n, i], device(-dx, -dy, 0, dc),
+                )
+                copy.start()
+                d_copies.append(copy)
+
+    def state_grad(block):
+        if block == 0:
+            for q in range(4):
+                w_arrived(0, q)
+            for q in range(2):
+                w_arrived(2, q)
         rows = pl.ds(block * 256, 256)
-        dims = (((1,), (1,)), ((), ()))
-        own, other = wr[0, j].reshape(512, KV), wr[1, j].reshape(512, KV)
+        own, other = wr[0, jy].reshape(512, KV), wr[1, jy].reshape(512, KV)
         value = lax.dot_general(k2[rows, 0:KV], own, dims, preferred_element_type=F32)
         value += lax.dot_general(k2[rows, KV:], other, dims, preferred_element_type=F32)
-        dxs[j, rows] = value.astype(BF16)
-        for i, (dx, dy, dc, row, n, slot, rel) in enumerate(ITEMS):
-            if slot // 256 != block:
-                continue
-            copy = remote(
-                dxs.at[j, pl.ds(slot, n)], dxr.at[rel - 1, j, pl.ds(row, n)],
-                d_send.at[r, i], d_recv.at[r, i], device(-dx, -dy, 0, dc),
-            )
-            copy.start()
-            d_copies.append(copy)
+        dxs[jy, rows] = value.astype(BF16)
+        send_back(0, jy, block * 256, block * 256 + 256, pl.ds(0, KV))
+
+    def state_grad_late(q):
+        if q > 1:
+            w_arrived(1, q)
+        landed(wr.at[1, jn, blocks[q]], w_recv.at[13 + q])
+        lanes = pl.ds(pl.multiple_of(blocks[q] * 128, 128), 128)
+        for block in range(2):
+            rows = pl.ds(block * 512, 512)
+            value = lax.dot_general(k2[rows, 0:KV], wr[0, jn, blocks[q]], dims, preferred_element_type=F32)
+            value += lax.dot_general(k2[rows, KV:], wr[1, jn, blocks[q]], dims, preferred_element_type=F32)
+            dxs[jn, rows, lanes] = value.astype(BF16)
+        send_back(1 + q, jn, 0, GROUP, lanes)
 
     def chunk(target):
         target = lax.rem(target + NZ, NZ)
@@ -263,17 +283,17 @@
     for half in range(2):
         chain(0, 1, half)
     for q in range(4):
-        w_along_y(q)
+        w_other_half(q)
 
     background = {
-        (1, 0): lambda: (w_all(0), state_grad(0, 0)),
-        (1, 2): lambda: state_grad(0, 1),
-        (2, 0): lambda: state_grad(0, 2),
-        (2, 2): lambda: state_grad(0, 3),
-        (4, 0): lambda: (w_all(1), state_grad(1, 0)),
-        (4, 2): lambda: state_grad(1, 1),
-        (5, 0): lambda: state_grad(1, 2),
-        (5, 2): lambda: state_grad(1, 3),
+        (1, 0): lambda: state_grad(0),
+        (1, 1): lambda: state_grad(1),
+        (1, 2): lambda: state_grad(2),
+        (1, 3): lambda: state_grad(3),
+        (2, 3): lambda: state_grad_late(0),
+        (3, 3): lambda: state_grad_late(1),
+        (4, 3): lambda: state_grad_late(2),
+        (5, 3): lambda: state_grad_late(3),
     }
     for step in range(1, 8):
         for unit in range(4):
@@ -326,11 +346,11 @@
     return pl.pallas_call(
         kernel,
         out_shape=(
-            jax.ShapeDtypeStruct((ROWS, WIDTH), BF16),
+            pltpu.VMEM((ROWS, WIDTH), BF16),
             jax.ShapeDtypeStruct((32, KV), F32),
         ),
         in_specs=[any_spec] * 4,
-        out_specs=(any_spec, vmem),
+        out_specs=(vmem, vmem),
         scratch_shapes=[
             pltpu.VMEM((7, 2, ROWS, KV), BF16),
             pltpu.VMEM((2, GROUP, KV), BF16),
@@ -352,8 +372,8 @@
             dma((10,)),
             dma((17,)),
             dma((17,)),
-            dma((2, len(ITEMS))),
-            dma((2, len(ITEMS))),
+            dma((5, len(ITEMS))),
+            dma((5, len(ITEMS))),
             dma((2, 8, 2, 2, 2)),
             dma((2, 8, 2, 2, 2)),
             dma((3,)),

time: 81.8 us -> 78.5 us (0.960)
  the two profiles are of different devices: /device:TPU:6 before, /device:TPU:32 now
where the time goes in v3:
time: 78.5 us; the launch traced here: 78.3 us
  Pallas kernels  75.7 us (96%)
  local copies, waits for them, and re-layouts  1.96 us (2%)
    pallas_call x1, Pallas kernels, body(): pl.pallas_call(kernel, out_shape=(pltpu.VMEM((ROWS, WIDTH), BF16), jax.Sh...  75.7 us
    unnamed x4, local copies, waits for them, and re-layouts  1.96 us

profile of v3, /device:TPU:32, one launch (start us, length us, event | category | flops | bytes accessed | tf_op | source)
XLA Modules:
  0.0 78.3 jit_solution(8872549155506531416)
XLA Ops:
  0.6 75.7 %exchange.1 = (bf16[128,8192]{1,0:T(8,128)(2,1)S(1)}, f32[32,512]{1,0:T(8,128)}) custom-call(bf16[128,8192]{1,0:T(8,128)(2,1)} %x_ref.1, bf16[128,512]{1,0:T(8,128)(2,1)} %k_ref.1, s32[1,128]{1,0:T(1,128)} %bitcast.1, bf16[512,512]{1,0:T(8,128)(2,1)} %w_ref.1), custom_call_target="tpu_custom_call" | custom-call | flops 4294967296 | bytes 5242880 | tf_op jit(solution)/shard_map/exchange/pallas_call | solution.py:346
  76.3 0.0 copy-start
  76.4 1.3 %copy.8 = bf16[128,8192]{1,0:T(8,128)(2,1)} copy(bf16[128,8192]{1,0:T(8,128)(2,1)S(1)} %get-tuple-element.2) | data formatting | bytes 4194304
  77.7 0.0 copy-done
  77.7 0.6 copy.9
Async XLA Ops:
  76.3 1.3 %copy-start = (f32[32,512]{1,0:T(8,128)S(1)}, f32[32,512]{1,0:T(8,128)}, u32[]{:S(2)}) copy-start(f32[32,512]{1,0:T(8,128)} %get-tuple-element.7) | copy-start | bytes 196612

commit v4 on v3

--- a/solution.py
+++ b/solution.py
@@ -104,7 +104,7 @@
 
     def w_along_z(r):
         j = (jy, jn, jy)[r]
-        for i, (dz, row, rows, _) in enumerate(ALONG_Z):
+        for i, (dz, row, rows, _) in enumerate(ALONG_Z[:2] if r == 1 else ALONG_Z):
             start = pl.multiple_of((py + 2 * j) * 128 + row, 64)
             dst = wr.at[r // 2, j, zl, pl.ds(row, rows)]
             copy = remote(
@@ -128,6 +128,12 @@
     )
 
     def w_other_half(q):
+        if q == 3:
+            w_arrived(0, q)
+            ref = wr.at[0, jy, blocks[q]]
+            copy = remote(ref, ref, w_send.at[17], w_recv.at[17], device(0, 2, 0, 0))
+            copy.start()
+            w_copies.append(copy)
         if q < 2:
             w_arrived(1, q)
             copy = remote(
@@ -223,7 +229,7 @@
 
     def state_grad(block):
         if block == 0:
-            for q in range(4):
+            for q in range(3):
                 w_arrived(0, q)
             for q in range(2):
                 w_arrived(2, q)
@@ -235,8 +241,10 @@
         send_back(0, jy, block * 256, block * 256 + 256, pl.ds(0, KV))
 
     def state_grad_late(q):
-        if q > 1:
+        if q == 2:
             w_arrived(1, q)
+        if q == 3:
+            landed(wr.at[0, jn, blocks[q]], w_recv.at[17])
         landed(wr.at[1, jn, blocks[q]], w_recv.at[13 + q])
         lanes = pl.ds(pl.multiple_of(blocks[q] * 128, 128), 128)
         for block in range(2):
@@ -265,7 +273,7 @@
                 value += codes[...].astype(F32) * scale[0:1, 0:1]
             top = jnp.maximum(jnp.max(jnp.abs(value), keepdims=True), 1e-30)
             codes[...] = jnp.round(value * (TOP / top)).astype(I32).astype(I16)
-            scale[...] = jnp.broadcast_to(top * (1.0 / TOP), (8, 128))
+            scale[...] = jnp.broadcast_to(top * (1.0 / TOP), (1, 128))
             to, copies = device(0, 0, dz, 0), []
             for i, ref in enumerate((units, sums)):
                 copy = remote(
@@ -360,7 +368,7 @@
             pltpu.VMEM((2, 2, ZL, 128, KV), BF16),
             pltpu.VMEM((2, ZL, ZH, 32, 2 * KV), F32),
             pltpu.VMEM((2, 9, 2, 2, UNIT, 2 * KV), I16),
-            pltpu.VMEM((2, 9, 2, 2, 8, 128), F32),
+            pltpu.VMEM((2, 9, 2, 2, 1, 128), F32),
             pltpu.VMEM((2, GROUP, KV), BF16),
             pltpu.VMEM((7, 2, ROWS, KV), BF16),
             pltpu.VMEM((3, 32, KV), F32),
@@ -370,8 +378,8 @@
             dma((2, len(ITEMS))),
             dma((10,)),
             dma((10,)),
-            dma((17,)),
-            dma((17,)),
+            dma((18,)),
+            dma((18,)),
             dma((5, len(ITEMS))),
             dma((5, len(ITEMS))),
             dma((2, 8, 2, 2, 2)),

time: 78.5 us -> 76.8 us (0.978)
  the two profiles are of different devices: /device:TPU:32 before, /device:TPU:6 now
where the time goes in v4:
time: 76.8 us; the launch traced here: 75.6 us
  Pallas kernels  73 us (95%)
  local copies, waits for them, and re-layouts  1.96 us (3%)
    pallas_call x1, Pallas kernels, body(): pl.pallas_call(kernel, out_shape=(pltpu.VMEM((ROWS, WIDTH), BF16), jax.Sh...  73 us
    unnamed x4, local copies, waits for them, and re-layouts  1.96 us

profile of v4, /device:TPU:6, one launch (start us, length us, event | category | flops | bytes accessed | tf_op | source)
XLA Modules:
  0.0 75.6 jit_solution(7093482053250308972)
XLA Ops:
  0.6 73.0 %exchange.1 = (bf16[128,8192]{1,0:T(8,128)(2,1)S(1)}, f32[32,512]{1,0:T(8,128)}) custom-call(bf16[128,8192]{1,0:T(8,128)(2,1)} %x_ref.1, bf16[128,512]{1,0:T(8,128)(2,1)} %k_ref.1, s32[1,128]{1,0:T(1,128)} %bitcast.1, bf16[512,512]{1,0:T(8,128)(2,1)} %w_ref.1), custom_call_target="tpu_custom_call" | custom-call | flops 4294967296 | bytes 5242880 | tf_op jit(solution)/shard_map/exchange/pallas_call | solution.py:354
  73.6 0.0 copy-start
  73.6 1.3 %copy.8 = bf16[128,8192]{1,0:T(8,128)(2,1)} copy(bf16[128,8192]{1,0:T(8,128)(2,1)S(1)} %get-tuple-element.2) | data formatting | bytes 4194304
  75.0 0.0 copy-done
  75.0 0.6 copy.9
Async XLA Ops:
  73.6 1.3 %copy-start = (f32[32,512]{1,0:T(8,128)S(1)}, f32[32,512]{1,0:T(8,128)}, u32[]{:S(2)}) copy-start(f32[32,512]{1,0:T(8,128)} %get-tuple-element.7) | copy-start | bytes 196612

commit v5 on v4

--- a/solution.py
+++ b/solution.py
@@ -147,6 +147,9 @@
         copy.start()
         w_copies.append(copy)
 
+    w_across.start()
+    w_copies.append(w_across)
+    w_along_z(0)
     k_copies = []
     for i, (dx, dy, row, rows, slot) in enumerate(DIRS):
         copy = remote(
@@ -161,10 +164,6 @@
     x_copies = ([], [])
     staged = set()
     for o in range(2):
-        if o == 0:
-            w_across.start()
-            w_copies.append(w_across)
-            w_along_z(0)
         for i, (dx, dy, dc, row, rows, slot, rel) in enumerate(ITEMS):
             if rel not in staged:
                 staged.add(rel)
@@ -185,6 +184,9 @@
         kr.at[pl.ds(128, 384)], kr.at[pl.ds(640, 384)], k_send.at[9], k_recv.at[9], device(0, 0, 0, 1)
     )
     relay.start()
+    w_across.wait_recv()
+    w_along_z(2)
+    w_along_z(1)
     k_own.wait_recv()
     own_kind = lax.div(x, 2).astype(F32)
 
@@ -201,9 +203,6 @@
     relay.wait_recv()
     for i in range(5, 8):
         masked(i)
-    w_across.wait_recv()
-    w_along_z(2)
-    w_along_z(1)
 
     def partial(o):
         for copy in x_copies[o]:

time: 76.8 us -> 76.8 us (level)
  no operation moved by 1% of the time
where the time goes in v5:
time: 76.8 us; the launch traced here: 75.6 us
  Pallas kernels  73 us (95%)
  local copies, waits for them, and re-layouts  1.96 us (3%)
    pallas_call x1, Pallas kernels, body(): pl.pallas_call(kernel, out_shape=(pltpu.VMEM((ROWS, WIDTH), BF16), jax.Sh...  73 us
    unnamed x4, local copies, waits for them, and re-layouts  1.96 us

profile of v5, /device:TPU:6, one launch (start us, length us, event | category | flops | bytes accessed | tf_op | source)
XLA Modules:
  0.0 75.6 jit_solution(3974853529791487646)
XLA Ops:
  0.6 73.0 %exchange.1 = (bf16[128,8192]{1,0:T(8,128)(2,1)S(1)}, f32[32,512]{1,0:T(8,128)}) custom-call(bf16[128,8192]{1,0:T(8,128)(2,1)} %x_ref.1, bf16[128,512]{1,0:T(8,128)(2,1)} %k_ref.1, s32[1,128]{1,0:T(1,128)} %bitcast.1, bf16[512,512]{1,0:T(8,128)(2,1)} %w_ref.1), custom_call_target="tpu_custom_call" | custom-call | flops 4294967296 | bytes 5242880 | tf_op jit(solution)/shard_map/exchange/pallas_call | solution.py:353
  73.7 0.0 copy-start
  73.7 1.3 %copy.8 = bf16[128,8192]{1,0:T(8,128)(2,1)} copy(bf16[128,8192]{1,0:T(8,128)(2,1)S(1)} %get-tuple-element.2) | data formatting | bytes 4194304
  75.0 0.0 copy-done
  75.0 0.6 copy.9
Async XLA Ops:
  73.7 1.3 %copy-start = (f32[32,512]{1,0:T(8,128)S(1)}, f32[32,512]{1,0:T(8,128)}, u32[]{:S(2)}) copy-start(f32[32,512]{1,0:T(8,128)} %get-tuple-element.7) | copy-start | bytes 196612
